TPU v7x, 32 devices: a whole 2x2x4 slice. The times are simulated.
32 devices in a mesh: groups: 2 (over x), ao: 16 (over z, y, core).
Axes of the slice: x: 2, y: 2, z: 4, core: 2. Of those that a mesh axis runs over, the one named last changes fastest.
Arguments:
- b_factor: bfloat16 [512, 4, 8192], P('ao', 'groups'), parts along dimension 1, may hold values from -2.5 to 2.5
- tile_pairs: int32 [512, 2], P(('groups', 'ao')), parts along dimension 0, may hold values from 0 to 63, as said below
- tile_count: int32 [32], P(('groups', 'ao')), parts along dimension 0, may hold values from 3 to 16, as said below
Outputs:
- k_tiles: float32 [512, 128, 128], P(('groups', 'ao')), parts along dimension 0
There are 2 independent parts, one for each index of `groups`. A program takes and returns all parts, laid end to end along the dimension named above; each array names one. Nothing has to cross between parts.
Inputs may be any that keep to these rules, and one draw needn't show every extreme that they name: `tile_pairs`: each row names a row block no larger than its column block. The live rows of a device name exactly 6 distinct blocks; the live rows of devices 2k and 2k+1 together name 10 consecutive blocks. Rows that are not live also hold valid block numbers. `tile_count`: some device fills all 16 slots.
All inputs are finite; a program needn't handle non-finite values.
Results may differ from a plain program's by a relative error of at most 0.0003.
Values may be sent and summed in bfloat16 or wider, within the bound.
A program may use at most 64 MiB of HBM per device.

v0:
```python
import jax
import jax.numpy as jnp
from jax import lax
from jax.sharding import PartitionSpec as P

BLK = 128
WINDOW = 10


def shards(b_factor, tile_pairs, tile_count):
    devices = lax.axis_size("ao")
    myself = lax.axis_index("ao")
    slot_total = tile_pairs.shape[0]
    occ_local, auxiliary, orbitals = b_factor.shape
    block_total = orbitals // BLK
    listed, counted = (
        lax.all_gather(tile_pairs, "ao", axis=0, tiled=True),
        lax.all_gather(tile_count, "ao", axis=0, tiled=True),
    )
    listed = listed.reshape(devices, slot_total, 2)
    slot_range = jnp.arange(slot_total, dtype=jnp.int32)
    work_live = slot_range[None, :] < counted[:, None]
    my_pairs = listed[myself]
    my_live = work_live[myself]
    capacity = WINDOW
    lowest = jnp.min(jnp.where(work_live[:, :, None], listed, block_total), axis=(1, 2))
    lowest = jnp.minimum(lowest, block_total - WINDOW)
    slot_blocks = lowest[:, None] + jnp.arange(WINDOW, dtype=jnp.int32)[None, :]
    my_slots = my_pairs - lowest[myself]
    block_view = b_factor.reshape(occ_local, auxiliary, block_total, BLK)
    picked = jnp.take(block_view, slot_blocks.reshape(-1), axis=2)
    picked = picked.reshape(occ_local, auxiliary, devices, capacity, BLK)
    arrived = lax.all_to_all(picked, "ao", split_axis=2, concat_axis=0, tiled=True)
    arrived = arrived.reshape(-1, capacity, BLK)

    def compute(slot_pair):
        left_block = lax.dynamic_index_in_dim(arrived, slot_pair[0], 1, keepdims=False)
        right_block = lax.dynamic_index_in_dim(arrived, slot_pair[1], 1, keepdims=False)
        return lax.dot_general(
            left_block, right_block, (((0,), (0,)), ((), ())), preferred_element_type=jnp.float32
        )

    def nothing(slot_pair):
        return jnp.zeros((BLK, BLK), jnp.float32)

    def one_tile(operands):
        slot_pair, live_flag = operands
        return lax.cond(live_flag, compute, nothing, slot_pair)

    results = lax.map(one_tile, (my_slots, my_live))
    return results


def solution(mesh):
    in_specs = (P("ao", "groups", None), P(("groups", "ao"), None), P(("groups", "ao")))
    out_specs = P(("groups", "ao"), None, None)
    return jax.shard_map(shards, mesh=mesh, in_specs=in_specs, out_specs=out_specs, check_vma=False)
```

profile of v0, /device:TPU:13, one launch (start us, length us, event | category | flops | bytes accessed | tf_op | source)
XLA Modules:
  0.0 214.4 jit_solution(1677174470879150203)
XLA Ops:
  0.7 1.2 dynamic-slice
  1.9 0.8 dynamic-update-slice
  2.7 7.9 %all-reduce = s32[16]{0:T(128)S(1)} all-reduce(s32[16]{0:T(128)S(1)} %dynamic-update-slice), channel_id=1, replica_groups=mesh['groups'=2,'ao'=16] {'ao'}, use_global_device_ids=true, to_apply=%add | all-reduce | flops 16 | bytes 128
  10.7 19.9 %all-gather = s32[16,16,2]{1,2,0:T(2,128)S(1)} all-gather(s32[1,16,2]{1,2,0:T(2,128)} %bitcast.34), channel_id=1, replica_groups=mesh['groups'=2,'ao'=16] {'ao'}, dimensions={0}, use_global_device_ids=true | all-gather | bytes 2176 | tf_op jit(solution)/shard_map/all_gather | solution.py:17
  31.2 1.9 reshape.105
  33.0 0.7 copy.19
  33.7 2.5 %gather_fusion = bf16[160,32,2,128]{3,1,2,0:T(8,128)(2,1)} fusion(bf16[32,2,64,128]{3,0,2,1:T(8,128)(2,1)S(1)} %copy.19, s32[1024]{0:T(1024)S(1)} %pad_clamp_fusion), kind=kCustom, calls=%fused_computation | custom fusion | bytes 5243520 | tf_op jit(solution)/shard_map/jit(_take)/gather | solution.py:31
  36.3 2.2 %copy.20 = bf16[32,2,160,128]{3,0,2,1:T(8,128)(2,1)S(1)} copy(bf16[32,2,160,128]{3,0,1,2:T(8,128)(2,1)} %bitcast.31) | data formatting | bytes 5242880 | tf_op jit(solution)/shard_map/jit(_take)/gather | solution.py:31
  38.8 2.0 copy.21
  40.8 7.0 %all-to-all-start = ((bf16[32,2,16,10,128]{4,0,3,1,2:T(8,128)(2,1)}), bf16[32,2,16,10,128]{4,0,3,1,2:T(8,128)(2,1)S(1)}, u32[]{:S(2)}, u32[]{:S(2)}) async-start(bf16[32,2,16,10,128]{4,0,3,1,2:T(8,128)(2,1)} %copy.21), calls=%async_computation | async-start | bytes 5242880 | tf_op jit(solution)/shard_map/all_to_all | solution.py:33
  47.8 0.7 dynamic_slice.31
  48.5 0.6 fusion.5
  49.1 57.4 %all-to-all-done = bf16[32,2,16,10,128]{4,0,3,1,2:T(8,128)(2,1)S(1)} async-done(((bf16[32,2,16,10,128]{4,0,3,1,2:T(8,128)(2,1)}), bf16[32,2,16,10,128]{4,0,3,1,2:T(8,128)(2,1)S(1)}, u32[]{:S(2)}, u32[]{:S(2)}) %all-to-all-start) | async-done | bytes 2621472 | tf_op jit(solution)/shard_map/all_to_all | solution.py:33
  106.5 1.5 copy-done
  108.0 5.8 %copy.22 = bf16[16,32,2,1,10,128]{5,2,1,0,4,3:T(2,128)(2,1)S(1)} copy(bf16[16,32,2,1,10,128]{5,1,4,2,0,3:T(8,128)(2,1)} %bitcast.30) | data formatting | bytes 5242880 | tf_op jit(solution)/shard_map/all_to_all | solution.py:33
  113.8 100.7 %while.10 = (s32[]{:T(128)}, f32[16,128,128]{2,1,0:T(8,128)}, pred[16]{0:T(512)(128)(4,1)S(1)}, s32[16,2]{0,1:T(2,128)S(1)}, bf16[1024,10,128]{2,0,1:T(8,128)(2,1)S(1)}, /*index=5*/s32[]{:T(128)}) while((s32[]{:T(128)}, f32[16,128,128]{2,1,0:T(8,128)}, pred[16]{0:T(512)(128)(4,1)S(1)}, s32[16,2]{0,1:T(2,128)S(1)}, ...), condition=%wide.region_5.6_spmd, body=%wide.region_2.5_spmd.sunk | while | flops 33554440 | bytes 721632 | solution.py:50
  113.8 0.6 dynamic_slice.43
  114.9 4.5 %conditional.2 = (f32[1,128,128]{2,1,0:T(8,128)S(1)}) conditional(s32[]{:T(128)} %bitcast.28, () %tuple.31, (s32[16,2]{0,1:T(2,128)S(1)}, s32[]{:T(128)}, bf16[1024,10,128]{2,0,1:T(8,128)(2,1)S(1)}) %tuple.32), branch_computations={%region_3.3_spmd, %region_4.4_spmd} | conditional | flops 33554440 | bytes 589944 | solution.py:48
  119.5 0.6 constant_dynamic-update-slice_fusion.2
  120.1 0.6 dynamic_slice.43
  121.2 4.5 %conditional.2 = (f32[1,128,128]{2,1,0:T(8,128)S(1)}) conditional(s32[]{:T(128)} %bitcast.28, () %tuple.31, (s32[16,2]{0,1:T(2,128)S(1)}, s32[]{:T(128)}, bf16[1024,10,128]{2,0,1:T(8,128)(2,1)S(1)}) %tuple.32), branch_computations={%region_3.3_spmd, %region_4.4_spmd} | conditional | flops 33554440 | bytes 589944 | solution.py:48
  125.7 0.6 constant_dynamic-update-slice_fusion.2
  126.4 0.6 dynamic_slice.43
  127.5 4.5 %conditional.2 = (f32[1,128,128]{2,1,0:T(8,128)S(1)}) conditional(s32[]{:T(128)} %bitcast.28, () %tuple.31, (s32[16,2]{0,1:T(2,128)S(1)}, s32[]{:T(128)}, bf16[1024,10,128]{2,0,1:T(8,128)(2,1)S(1)}) %tuple.32), branch_computations={%region_3.3_spmd, %region_4.4_spmd} | conditional | flops 33554440 | bytes 589944 | solution.py:48
  132.0 0.6 constant_dynamic-update-slice_fusion.2
  132.7 0.6 dynamic_slice.43
  133.8 4.5 %conditional.2 = (f32[1,128,128]{2,1,0:T(8,128)S(1)}) conditional(s32[]{:T(128)} %bitcast.28, () %tuple.31, (s32[16,2]{0,1:T(2,128)S(1)}, s32[]{:T(128)}, bf16[1024,10,128]{2,0,1:T(8,128)(2,1)S(1)}) %tuple.32), branch_computations={%region_3.3_spmd, %region_4.4_spmd} | conditional | flops 33554440 | bytes 589944 | solution.py:48
  138.3 0.6 constant_dynamic-update-slice_fusion.2
  139.0 0.6 dynamic_slice.43
  140.1 4.5 %conditional.2 = (f32[1,128,128]{2,1,0:T(8,128)S(1)}) conditional(s32[]{:T(128)} %bitcast.28, () %tuple.31, (s32[16,2]{0,1:T(2,128)S(1)}, s32[]{:T(128)}, bf16[1024,10,128]{2,0,1:T(8,128)(2,1)S(1)}) %tuple.32), branch_computations={%region_3.3_spmd, %region_4.4_spmd} | conditional | flops 33554440 | bytes 589944 | solution.py:48
  144.6 0.6 constant_dynamic-update-slice_fusion.2
  145.3 0.6 dynamic_slice.43
  146.4 4.5 %conditional.2 = (f32[1,128,128]{2,1,0:T(8,128)S(1)}) conditional(s32[]{:T(128)} %bitcast.28, () %tuple.31, (s32[16,2]{0,1:T(2,128)S(1)}, s32[]{:T(128)}, bf16[1024,10,128]{2,0,1:T(8,128)(2,1)S(1)}) %tuple.32), branch_computations={%region_3.3_spmd, %region_4.4_spmd} | conditional | flops 33554440 | bytes 589944 | solution.py:48
  150.9 0.6 constant_dynamic-update-slice_fusion.2
  151.5 0.6 dynamic_slice.43
  152.7 4.5 %conditional.2 = (f32[1,128,128]{2,1,0:T(8,128)S(1)}) conditional(s32[]{:T(128)} %bitcast.28, () %tuple.31, (s32[16,2]{0,1:T(2,128)S(1)}, s32[]{:T(128)}, bf16[1024,10,128]{2,0,1:T(8,128)(2,1)S(1)}) %tuple.32), branch_computations={%region_3.3_spmd, %region_4.4_spmd} | conditional | flops 33554440 | bytes 589944 | solution.py:48
  157.2 0.6 constant_dynamic-update-slice_fusion.2
  157.8 0.6 dynamic_slice.43
  159.0 4.5 %conditional.2 = (f32[1,128,128]{2,1,0:T(8,128)S(1)}) conditional(s32[]{:T(128)} %bitcast.28, () %tuple.31, (s32[16,2]{0,1:T(2,128)S(1)}, s32[]{:T(128)}, bf16[1024,10,128]{2,0,1:T(8,128)(2,1)S(1)}) %tuple.32), branch_computations={%region_3.3_spmd, %region_4.4_spmd} | conditional | flops 33554440 | bytes 589944 | solution.py:48
  163.5 0.6 constant_dynamic-update-slice_fusion.2
  164.1 0.6 dynamic_slice.43
  165.3 4.5 %conditional.2 = (f32[1,128,128]{2,1,0:T(8,128)S(1)}) conditional(s32[]{:T(128)} %bitcast.28, () %tuple.31, (s32[16,2]{0,1:T(2,128)S(1)}, s32[]{:T(128)}, bf16[1024,10,128]{2,0,1:T(8,128)(2,1)S(1)}) %tuple.32), branch_computations={%region_3.3_spmd, %region_4.4_spmd} | conditional | flops 33554440 | bytes 589944 | solution.py:48
  169.8 0.6 constant_dynamic-update-slice_fusion.2
  170.4 0.6 dynamic_slice.43
  171.6 4.5 %conditional.2 = (f32[1,128,128]{2,1,0:T(8,128)S(1)}) conditional(s32[]{:T(128)} %bitcast.28, () %tuple.31, (s32[16,2]{0,1:T(2,128)S(1)}, s32[]{:T(128)}, bf16[1024,10,128]{2,0,1:T(8,128)(2,1)S(1)}) %tuple.32), branch_computations={%region_3.3_spmd, %region_4.4_spmd} | conditional | flops 33554440 | bytes 589944 | solution.py:48
  176.1 0.6 constant_dynamic-update-slice_fusion.2
  176.7 0.6 dynamic_slice.43
  177.8 4.5 %conditional.2 = (f32[1,128,128]{2,1,0:T(8,128)S(1)}) conditional(s32[]{:T(128)} %bitcast.28, () %tuple.31, (s32[16,2]{0,1:T(2,128)S(1)}, s32[]{:T(128)}, bf16[1024,10,128]{2,0,1:T(8,128)(2,1)S(1)}) %tuple.32), branch_computations={%region_3.3_spmd, %region_4.4_spmd} | conditional | flops 33554440 | bytes 589944 | solution.py:48
  182.4 0.6 constant_dynamic-update-slice_fusion.2
  183.0 0.6 dynamic_slice.43
  184.1 4.5 %conditional.2 = (f32[1,128,128]{2,1,0:T(8,128)S(1)}) conditional(s32[]{:T(128)} %bitcast.28, () %tuple.31, (s32[16,2]{0,1:T(2,128)S(1)}, s32[]{:T(128)}, bf16[1024,10,128]{2,0,1:T(8,128)(2,1)S(1)}) %tuple.32), branch_computations={%region_3.3_spmd, %region_4.4_spmd} | conditional | flops 33554440 | bytes 589944 | solution.py:48
  188.6 0.6 constant_dynamic-update-slice_fusion.2
  189.3 0.6 dynamic_slice.43
  190.4 4.5 %conditional.2 = (f32[1,128,128]{2,1,0:T(8,128)S(1)}) conditional(s32[]{:T(128)} %bitcast.28, () %tuple.31, (s32[16,2]{0,1:T(2,128)S(1)}, s32[]{:T(128)}, bf16[1024,10,128]{2,0,1:T(8,128)(2,1)S(1)}) %tuple.32), branch_computations={%region_3.3_spmd, %region_4.4_spmd} | conditional | flops 33554440 | bytes 589944 | solution.py:48
  194.9 0.6 constant_dynamic-update-slice_fusion.2
  195.6 0.6 dynamic_slice.43
  196.7 4.5 %conditional.2 = (f32[1,128,128]{2,1,0:T(8,128)S(1)}) conditional(s32[]{:T(128)} %bitcast.28, () %tuple.31, (s32[16,2]{0,1:T(2,128)S(1)}, s32[]{:T(128)}, bf16[1024,10,128]{2,0,1:T(8,128)(2,1)S(1)}) %tuple.32), branch_computations={%region_3.3_spmd, %region_4.4_spmd} | conditional | flops 33554440 | bytes 589944 | solution.py:48
  201.2 0.6 constant_dynamic-update-slice_fusion.2
  201.9 0.6 dynamic_slice.43
  203.0 4.5 %conditional.2 = (f32[1,128,128]{2,1,0:T(8,128)S(1)}) conditional(s32[]{:T(128)} %bitcast.28, () %tuple.31, (s32[16,2]{0,1:T(2,128)S(1)}, s32[]{:T(128)}, bf16[1024,10,128]{2,0,1:T(8,128)(2,1)S(1)}) %tuple.32), branch_computations={%region_3.3_spmd, %region_4.4_spmd} | conditional | flops 33554440 | bytes 589944 | solution.py:48
  207.5 0.6 constant_dynamic-update-slice_fusion.2
  208.2 0.6 dynamic_slice.43
  209.3 4.5 %conditional.2 = (f32[1,128,128]{2,1,0:T(8,128)S(1)}) conditional(s32[]{:T(128)} %bitcast.28, () %tuple.31, (s32[16,2]{0,1:T(2,128)S(1)}, s32[]{:T(128)}, bf16[1024,10,128]{2,0,1:T(8,128)(2,1)S(1)}) %tuple.32), branch_computations={%region_3.3_spmd, %region_4.4_spmd} | conditional | flops 33554440 | bytes 589944 | solution.py:48
  213.8 0.6 constant_dynamic-update-slice_fusion.2
  (66 shorter events, 15.3 us)
Async XLA Ops:
  40.8 65.6 %all-to-all-start = ((bf16[32,2,16,10,128]{4,0,3,1,2:T(8,128)(2,1)}), bf16[32,2,16,10,128]{4,0,3,1,2:T(8,128)(2,1)S(1)}, u32[]{:S(2)}, u32[]{:S(2)}) async-start(bf16[32,2,16,10,128]{4,0,3,1,2:T(8,128)(2,1)} %copy.21), calls=%async_computation | async-start | bytes 5242880 | tf_op jit(solution)/shard_map/all_to_all | solution.py:33
  106.5 1.5 copy-start
where the time goes:
time: 216 us; the launch traced here: 214 us
  loops' own time  66.9 us (31%)
  waiting for transfers between devices  57.4 us (27%)
  local copies, waits for them, and re-layouts  49.1 us (23%)
  blocking collectives  27.8 us (13%)
  starting transfers between devices  6.97 us (3%)
  matrix products  4.33 us (2%)
    another operation x16, loops' own time, one_tile(): return lax.cond(live_flag, compute, nothing, slot_pair)  57.7 us
    all_to_all x1, waiting for transfers between devices, shards(): lax.all_to_all(picked, 'ao', split_axis=2, concat_axis=0, tiled=True)  57.4 us
    all_gather x1, blocking collectives, shards(): lax.all_gather(tile_pairs, 'ao', axis=0, tiled=True)  19.9 us
    dynamic_slice x32, local copies, waits for them, and re-layouts, shards(): results = lax.map(one_tile, (my_slots, my_live))  10.5 us
    dynamic_update_slice x16, local copies, waits for them, and re-layouts, shards(): results = lax.map(one_tile, (my_slots, my_live))  10.2 us
    another operation x1, loops' own time, shards(): results = lax.map(one_tile, (my_slots, my_live))  9.19 us
    slice x16, local copies, waits for them, and re-layouts, compute(): slot_pair[0]  8.74 us
    unnamed x1, blocking collectives  7.88 us
  transfers between devices with their start and end apart: 1, of which 1 were waited for; matrix products, arithmetic and copies ran while one was open for 1% of the time, Pallas kernels for 0%

commit v1 on v0

v1 whole, which is shorter than its diff:
```python
import functools

import jax
import jax.numpy as jnp
from jax import lax
from jax.experimental import pallas as pl
from jax.experimental.pallas import tpu as pltpu
from jax.sharding import PartitionSpec as P

BLK = 128
WINDOW = 10
HALF = WINDOW // 2
MESH = pl.DeviceIdType.MESH


def partner(chip, offset):
    bit = 1
    while bit <= offset:
        if offset & bit:
            chip = chip + bit - 2 * bit * (chip // bit % 2)
        bit *= 2
    return chip


def phase_lists(chips):
    far = list(range(chips - 1, 0, -1))
    return [[0] + far]


def kernel(chips, phases, pairs_ref, count_ref, b_ref, out_ref, note, notes, send, *rest):
    recvs = rest[:len(phases)]
    note_send, note_recv, data_send, data_recv, pass_send, pass_recv = rest[len(phases):]
    me = lax.axis_index("ao")
    chip, core = me // 2, me % 2
    sibling = me + 1 - 2 * core
    devices = 2 * chips
    slots = pairs_ref.shape[0]
    block_total = b_ref.shape[0]
    where_of = {d: (p, i) for p, group in enumerate(phases) for i, d in enumerate(group)}

    barrier = pltpu.get_barrier_semaphore()

    def greet(step, carry):
        other = lax.rem(me + step, devices)
        pl.semaphore_signal(barrier, inc=1, device_id={"ao": other}, device_id_type=MESH)
        return carry

    lax.fori_loop(1, devices, greet, 0)

    count = count_ref[0]
    lowest = jnp.int32(block_total - WINDOW)
    for t in range(slots):
        lowest = jnp.minimum(lowest, jnp.where(t < count, pairs_ref[t, 0], block_total - WINDOW))
    note[...] = jnp.full(note.shape, lowest, jnp.int32)
    notes[me] = note[...]
    pl.semaphore_wait(barrier, devices - 1)

    def note_copy(step, sender):
        other = lax.rem(me + step, devices)
        return pltpu.make_async_remote_copy(
            src_ref=note, dst_ref=notes.at[sender], send_sem=note_send.at[step],
            recv_sem=note_recv.at[step], device_id={"ao": other}, device_id_type=MESH)

    def start_note(step, carry):
        note_copy(step, me).start()
        return carry

    def end_note(step, carry):
        sender = lax.rem(me + devices - step, devices)
        note_copy(step, sender).wait_recv()
        return carry

    def end_note_send(step, carry):
        note_copy(step, me).wait_send()
        return carry

    lax.fori_loop(1, devices, start_note, 0)
    lax.fori_loop(1, devices, end_note, 0)

    def window_of(which):
        return jnp.maximum(jnp.min(notes[pl.ds(2 * which, 2)]), 0)

    def data_copy(d, sender_core, c):
        p, i = where_of[d]
        return pltpu.make_async_remote_copy(
            src_ref=send.at[d, c], dst_ref=recvs[p].at[i, sender_core, pl.ds(HALF * c, HALF)],
            send_sem=data_send.at[d, c], recv_sem=data_recv.at[d, sender_core],
            device_id={"ao": 2 * partner(chip, d) + c}, device_id_type=MESH)

    def pass_copy(d, s, c):
        p, i = where_of[d]
        part = recvs[p].at[i, s, pl.ds(HALF * c, HALF)]
        return pltpu.make_async_remote_copy(
            src_ref=part, dst_ref=part, send_sem=pass_send.at[d, s], recv_sem=pass_recv.at[d, s],
            device_id={"ao": sibling}, device_id_type=MESH)

    order = [d for group in phases for d in group if d]
    for d in order:
        low = window_of(partner(chip, d))
        for c in range(2):
            send[d, c] = b_ref[pl.ds(low + HALF * c, HALF)]
            data_copy(d, core, c).start()

    my_low = window_of(chip)
    p0, i0 = where_of[0]
    recvs[p0][i0, core] = b_ref[pl.ds(my_low, WINDOW)]

    def own_copy(s):
        part = recvs[p0].at[i0, s]
        return pltpu.make_async_remote_copy(
            src_ref=part, dst_ref=part, send_sem=pass_send.at[0, 0], recv_sem=pass_recv.at[0, 0],
            device_id={"ao": sibling}, device_id_type=MESH)

    own_copy(core).start()
    for d in order:
        for s in range(2):
            data_copy(d, s, core).wait_recv()
            pass_copy(d, s, core).start()

    for p, group in enumerate(phases):
        for d in group:
            if d == 0:
                own_copy(1 - core).wait_recv()
            else:
                for s in range(2):
                    pass_copy(d, s, 1 - core).wait_recv()

        def tile(t, carry):
            left = jnp.clip(pairs_ref[t, 0] - my_low, 0, WINDOW - 1)
            right = jnp.clip(pairs_ref[t, 1] - my_low, 0, WINDOW - 1)
            a = recvs[p][:, :, left].reshape(-1, BLK)
            b = recvs[p][:, :, right].reshape(-1, BLK)
            value = lax.dot_general(a, b, (((0,), (0,)), ((), ())), preferred_element_type=jnp.float32)
            if p:
                value = value + out_ref[t]
            if p == len(phases) - 1:
                value = jnp.where(t < count, value, 0.0)
            out_ref[t] = value
            return carry

        lax.fori_loop(0, slots, tile, 0)

    lax.fori_loop(1, devices, end_note_send, 0)
    own_copy(core).wait_send()
    for d in order:
        for c in range(2):
            data_copy(d, core, c).wait_send()
            pass_copy(d, c, core).wait_send()


def shards(b_factor, tile_pairs, tile_count):
    devices = lax.axis_size("ao")
    chips = devices // 2
    occ_local, auxiliary, orbitals = b_factor.shape
    depth = occ_local * auxiliary
    block_total = orbitals // BLK
    slots = tile_pairs.shape[0]
    blocks = b_factor.reshape(depth, block_total, BLK).transpose(1, 0, 2)
    phases = phase_lists(chips)
    return pl.pallas_call(
        functools.partial(kernel, chips, phases),
        out_shape=jax.ShapeDtypeStruct((slots, BLK, BLK), jnp.float32),
        in_specs=[
            pl.BlockSpec(memory_space=pltpu.SMEM),
            pl.BlockSpec(memory_space=pltpu.SMEM),
            pl.BlockSpec(memory_space=pltpu.VMEM),
        ],
        out_specs=pl.BlockSpec(memory_space=pltpu.VMEM),
        scratch_shapes=[
            pltpu.VMEM((8, BLK), jnp.int32),
            pltpu.VMEM((devices, 8, BLK), jnp.int32),
            pltpu.VMEM((chips, 2, HALF, depth, BLK), jnp.bfloat16),
            *[pltpu.VMEM((len(group), 2, WINDOW, depth, BLK), jnp.bfloat16) for group in phases],
            pltpu.SemaphoreType.DMA((devices,)),
            pltpu.SemaphoreType.DMA((devices,)),
            pltpu.SemaphoreType.DMA((chips, 2)),
            pltpu.SemaphoreType.DMA((chips, 2)),
            pltpu.SemaphoreType.DMA((chips, 2)),
            pltpu.SemaphoreType.DMA((chips, 2)),
        ],
        compiler_params=pltpu.CompilerParams(
            collective_id=0, has_side_effects=True, vmem_limit_bytes=32 * 1024 * 1024),
    )(tile_pairs, tile_count, blocks)


def solution(mesh):
    in_specs = (P("ao", "groups", None), P(("groups", "ao"), None), P(("groups", "ao")))
    out_specs = P(("groups", "ao"), None, None)
    return jax.shard_map(shards, mesh=mesh, in_specs=in_specs, out_specs=out_specs, check_vma=False)
```

time: 216 us -> 52.7 us (0.24)
  the two profiles are of different devices: /device:TPU:13 before, /device:TPU:0 now
where the time goes in v1:
time: 52.7 us; the launch traced here: 52.6 us
  Pallas kernels  48.3 us (92%)
  local copies, waits for them, and re-layouts  3.6 us (7%)
  between operations  0.69 us (1%)
    pallas_call x1, Pallas kernels, shards(): pl.pallas_call(functools.partial(kernel, chips, phases), out_shape=jax.Sh...  48.3 us
    reshape x2, local copies, waits for them, and re-layouts, shards(): blocks = b_factor.reshape(depth, block_total, BLK).transpose(1, 0, 2)  2.53 us
    unnamed x4, local copies, waits for them, and re-layouts  1.07 us

profile of v1, /device:TPU:0, one launch (start us, length us, event | category | flops | bytes accessed | tf_op | source)
XLA Modules:
  0.0 52.6 jit_solution(14207041186560774260)
XLA Ops:
  0.0 0.0 copy-start
  0.7 0.0 copy-done
  0.7 0.1 copy.6.pairs_ref
  0.8 1.8 %reshape.3 = bf16[64,64,128]{2,1,0:T(8,128)(2,1)S(1)} reshape(bf16[32,2,8192]{2,1,0:T(2,128)(2,1)} %param.3) | data formatting | bytes 2097152 | tf_op jit(solution)/shard_map/reshape | solution.py:158
  2.6 0.7 %copy.8 = bf16[64,64,128]{2,0,1:T(8,128)(2,1)S(1)} copy(bf16[64,64,128]{2,1,0:T(8,128)(2,1)S(1)} %reshape.3) | data formatting | bytes 2097152 | tf_op jit(solution)/shard_map/reshape | solution.py:158
  3.3 48.3 %shard_map.37 = f32[16,128,128]{2,1,0:T(8,128)S(1)} custom-call(s32[16,2]{1,0:T(8,128)S(1)} %copy.6.pairs_ref, s32[1]{0:T(128)S(6)} %copy.10.count_ref, bf16[64,64,128]{2,1,0:T(8,128)(2,1)S(1)} %bitcast.3), custom_call_target="tpu_custom_call" | custom-call | tf_op jit(solution)/shard_map/pallas_call | solution.py:160
  51.6 1.0 %copy.11 = f32[16,128,128]{2,1,0:T(8,128)} copy(f32[16,128,128]{2,1,0:T(8,128)S(1)} %shard_map.37) | data formatting | bytes 2097152
Async XLA Ops:
  0.0 0.7 %copy-start = (s32[16,2]{0,1:T(2,128)S(1)}, s32[16,2]{0,1:T(2,128)}, u32[]{:S(2)}) copy-start(s32[16,2]{0,1:T(2,128)} %param.4) | copy-start | bytes 388

commit v2 on v1

--- a/solution.py
+++ b/solution.py
@@ -23,8 +23,10 @@
 
 
 def phase_lists(chips):
-    far = list(range(chips - 1, 0, -1))
-    return [[0] + far]
+    half = chips // 2
+    quarter = half // 2
+    first = [0, half + quarter] + list(range(1, half))
+    return [first, [d for d in range(half, chips) if d not in first]]
 
 
 def kernel(chips, phases, pairs_ref, count_ref, b_ref, out_ref, note, notes, send, *rest):
@@ -34,7 +36,7 @@
     chip, core = me // 2, me % 2
     sibling = me + 1 - 2 * core
     devices = 2 * chips
-    slots = pairs_ref.shape[0]
+    slots = pairs_ref.shape[1]
     block_total = b_ref.shape[0]
     where_of = {d: (p, i) for p, group in enumerate(phases) for i, d in enumerate(group)}
 
@@ -50,32 +52,28 @@
     count = count_ref[0]
     lowest = jnp.int32(block_total - WINDOW)
     for t in range(slots):
-        lowest = jnp.minimum(lowest, jnp.where(t < count, pairs_ref[t, 0], block_total - WINDOW))
+        lowest = jnp.minimum(lowest, jnp.where(t < count, pairs_ref[0, t], block_total - WINDOW))
     note[...] = jnp.full(note.shape, lowest, jnp.int32)
     notes[me] = note[...]
     pl.semaphore_wait(barrier, devices - 1)
 
-    def note_copy(step, sender):
-        other = lax.rem(me + step, devices)
-        return pltpu.make_async_remote_copy(
-            src_ref=note, dst_ref=notes.at[sender], send_sem=note_send.at[step],
-            recv_sem=note_recv.at[step], device_id={"ao": other}, device_id_type=MESH)
-
-    def start_note(step, carry):
-        note_copy(step, me).start()
-        return carry
-
-    def end_note(step, carry):
-        sender = lax.rem(me + devices - step, devices)
-        note_copy(step, sender).wait_recv()
-        return carry
-
-    def end_note_send(step, carry):
-        note_copy(step, me).wait_send()
-        return carry
-
-    lax.fori_loop(1, devices, start_note, 0)
-    lax.fori_loop(1, devices, end_note, 0)
+    order = [d for group in phases for d in group if d]
+    peers = [(d, c) for d in order for c in range(2)]
+
+    def note_copy(d, c, sender):
+        return pltpu.make_async_remote_copy(
+            src_ref=note, dst_ref=notes.at[sender], send_sem=note_send.at[d, c],
+            recv_sem=note_recv.at[d, sender % 2], device_id={"ao": 2 * partner(chip, d) + c},
+            device_id_type=MESH)
+
+    def sibling_note(sender):
+        return pltpu.make_async_remote_copy(
+            src_ref=note, dst_ref=notes.at[sender], send_sem=note_send.at[0, 0],
+            recv_sem=note_recv.at[0, 0], device_id={"ao": sibling}, device_id_type=MESH)
+
+    for d, c in peers:
+        note_copy(d, c, me).start()
+    sibling_note(me).start()
 
     def window_of(which):
         return jnp.maximum(jnp.min(notes[pl.ds(2 * which, 2)]), 0)
@@ -94,13 +92,15 @@
             src_ref=part, dst_ref=part, send_sem=pass_send.at[d, s], recv_sem=pass_recv.at[d, s],
             device_id={"ao": sibling}, device_id_type=MESH)
 
-    order = [d for group in phases for d in group if d]
     for d in order:
+        for c in range(2):
+            note_copy(d, c, 2 * partner(chip, d) + c).wait_recv()
         low = window_of(partner(chip, d))
         for c in range(2):
             send[d, c] = b_ref[pl.ds(low + HALF * c, HALF)]
             data_copy(d, core, c).start()
 
+    sibling_note(sibling).wait_recv()
     my_low = window_of(chip)
     p0, i0 = where_of[0]
     recvs[p0][i0, core] = b_ref[pl.ds(my_low, WINDOW)]
@@ -112,22 +112,25 @@
             device_id={"ao": sibling}, device_id_type=MESH)
 
     own_copy(core).start()
-    for d in order:
-        for s in range(2):
-            data_copy(d, s, core).wait_recv()
-            pass_copy(d, s, core).start()
-
-    for p, group in enumerate(phases):
-        for d in group:
+
+    def pass_on(p):
+        for d in phases[p]:
+            for s in range(2):
+                if d:
+                    data_copy(d, s, core).wait_recv()
+                    pass_copy(d, s, core).start()
+
+    def multiply(p):
+        for d in phases[p]:
             if d == 0:
                 own_copy(1 - core).wait_recv()
             else:
                 for s in range(2):
                     pass_copy(d, s, 1 - core).wait_recv()
 
-        def tile(t, carry):
-            left = jnp.clip(pairs_ref[t, 0] - my_low, 0, WINDOW - 1)
-            right = jnp.clip(pairs_ref[t, 1] - my_low, 0, WINDOW - 1)
+        def tile(t):
+            left = jnp.clip(pairs_ref[0, t] - my_low, 0, WINDOW - 1)
+            right = jnp.clip(pairs_ref[1, t] - my_low, 0, WINDOW - 1)
             a = recvs[p][:, :, left].reshape(-1, BLK)
             b = recvs[p][:, :, right].reshape(-1, BLK)
             value = lax.dot_general(a, b, (((0,), (0,)), ((), ())), preferred_element_type=jnp.float32)
@@ -136,11 +139,19 @@
             if p == len(phases) - 1:
                 value = jnp.where(t < count, value, 0.0)
             out_ref[t] = value
-            return carry
-
-        lax.fori_loop(0, slots, tile, 0)
-
-    lax.fori_loop(1, devices, end_note_send, 0)
+
+        for t in range(slots):
+            tile(t)
+
+    pass_on(0)
+    for p in range(1, len(phases)):
+        pass_on(p)
+        multiply(p - 1)
+    multiply(len(phases) - 1)
+
+    sibling_note(me).wait_send()
+    for d, c in peers:
+        note_copy(d, c, me).wait_send()
     own_copy(core).wait_send()
     for d in order:
         for c in range(2):
@@ -167,12 +178,12 @@
         ],
         out_specs=pl.BlockSpec(memory_space=pltpu.VMEM),
         scratch_shapes=[
-            pltpu.VMEM((8, BLK), jnp.int32),
-            pltpu.VMEM((devices, 8, BLK), jnp.int32),
+            pltpu.VMEM((1, BLK), jnp.int32),
+            pltpu.VMEM((devices, 1, BLK), jnp.int32),
             pltpu.VMEM((chips, 2, HALF, depth, BLK), jnp.bfloat16),
             *[pltpu.VMEM((len(group), 2, WINDOW, depth, BLK), jnp.bfloat16) for group in phases],
-            pltpu.SemaphoreType.DMA((devices,)),
-            pltpu.SemaphoreType.DMA((devices,)),
+            pltpu.SemaphoreType.DMA((chips, 2)),
+            pltpu.SemaphoreType.DMA((chips, 2)),
             pltpu.SemaphoreType.DMA((chips, 2)),
             pltpu.SemaphoreType.DMA((chips, 2)),
             pltpu.SemaphoreType.DMA((chips, 2)),
@@ -180,7 +191,7 @@
         ],
         compiler_params=pltpu.CompilerParams(
             collective_id=0, has_side_effects=True, vmem_limit_bytes=32 * 1024 * 1024),
-    )(tile_pairs, tile_count, blocks)
+    )(tile_pairs.T, tile_count, blocks)
 
 
 def solution(mesh):

time: 52.7 us -> 44.3 us (0.84)
  the two profiles are of different devices: /device:TPU:0 before, /device:TPU:13 now
where the time goes in v2:
time: 44.3 us; the launch traced here: 44.1 us
  Pallas kernels  39.2 us (88%)
  local copies, waits for them, and re-layouts  4.18 us (9%)
  between operations  0.68 us (2%)
    pallas_call x1, Pallas kernels, shards(): pl.pallas_call(functools.partial(kernel, chips, phases), out_shape=jax.Sh...  39.2 us
    reshape x2, local copies, waits for them, and re-layouts, shards(): blocks = b_factor.reshape(depth, block_total, BLK).transpose(1, 0, 2)  2.53 us
    unnamed x3, local copies, waits for them, and re-layouts  1.65 us

profile of v2, /device:TPU:13, one launch (start us, length us, event | category | flops | bytes accessed | tf_op | source)
XLA Modules:
  0.0 44.1 jit_solution(7808420337593130466)
XLA Ops:
  0.7 1.9 %reshape.3 = bf16[64,64,128]{2,1,0:T(8,128)(2,1)S(1)} reshape(bf16[32,2,8192]{2,1,0:T(2,128)(2,1)} %param.3) | data formatting | bytes 2097152 | tf_op jit(solution)/shard_map/reshape | solution.py:169
  2.5 0.7 %copy.6 = bf16[64,64,128]{2,0,1:T(8,128)(2,1)S(1)} copy(bf16[64,64,128]{2,1,0:T(8,128)(2,1)S(1)} %reshape.3) | data formatting | bytes 2097152 | tf_op jit(solution)/shard_map/reshape | solution.py:169
  3.2 0.0 copy-start
  3.2 0.7 %copy-done = s32[16,2]{0,1:T(2,128)S(1)} copy-done((s32[16,2]{0,1:T(2,128)S(1)}, s32[16,2]{0,1:T(2,128)}, u32[]{:S(2)}) %copy-start) | copy-done | bytes 152
  3.9 39.2 %shard_map.37 = f32[16,128,128]{2,1,0:T(8,128)S(1)} custom-call(s32[2,16]{1,0:T(2,128)S(1)} %bitcast.5, s32[1]{0:T(128)S(6)} %copy.8.count_ref, bf16[64,64,128]{2,1,0:T(8,128)(2,1)S(1)} %bitcast.4), custom_call_target="tpu_custom_call" | custom-call | tf_op jit(solution)/shard_map/pallas_call | solution.py:171
  43.1 1.0 %copy.9 = f32[16,128,128]{2,1,0:T(8,128)} copy(f32[16,128,128]{2,1,0:T(8,128)S(1)} %shard_map.37) | data formatting | bytes 2097152
Async XLA Ops:
  3.2 0.7 %copy-start = (s32[16,2]{0,1:T(2,128)S(1)}, s32[16,2]{0,1:T(2,128)}, u32[]{:S(2)}) copy-start(s32[16,2]{0,1:T(2,128)} %param.4) | copy-start | bytes 388

commit v3 on v2

--- a/solution.py
+++ b/solution.py
@@ -23,15 +23,14 @@
 
 
 def phase_lists(chips):
-    half = chips // 2
-    quarter = half // 2
-    first = [0, half + quarter] + list(range(1, half))
+    half, quarter = chips // 2, chips // 4
+    first = [0, half + quarter] + list(range(1, half + 1))
     return [first, [d for d in range(half, chips) if d not in first]]
 
 
-def kernel(chips, phases, pairs_ref, count_ref, b_ref, out_ref, note, notes, send, *rest):
+def kernel(chips, phases, pairs_hbm, count_hbm, b_hbm, out_ref, pairs_ref, count_ref, raw, b_ref, note, notes, send, *rest):
     recvs = rest[:len(phases)]
-    note_send, note_recv, data_send, data_recv, pass_send, pass_recv = rest[len(phases):]
+    small_sem, raw_sem, note_send, note_recv, data_send, data_recv, pass_send, pass_recv = rest[len(phases):]
     me = lax.axis_index("ao")
     chip, core = me // 2, me % 2
     sibling = me + 1 - 2 * core
@@ -40,6 +39,12 @@
     block_total = b_ref.shape[0]
     where_of = {d: (p, i) for p, group in enumerate(phases) for i, d in enumerate(group)}
 
+    small = [
+        pltpu.make_async_copy(pairs_hbm, pairs_ref, small_sem.at[0]),
+        pltpu.make_async_copy(count_hbm, count_ref, small_sem.at[1]),
+    ]
+    for copy in small:
+        copy.start()
     barrier = pltpu.get_barrier_semaphore()
 
     def greet(step, carry):
@@ -48,7 +53,11 @@
         return carry
 
     lax.fori_loop(1, devices, greet, 0)
-
+    fetch = pltpu.make_async_copy(b_hbm, raw, raw_sem)
+    fetch.start()
+
+    for copy in small:
+        copy.wait()
     count = count_ref[0]
     lowest = jnp.int32(block_total - WINDOW)
     for t in range(slots):
@@ -74,6 +83,10 @@
     for d, c in peers:
         note_copy(d, c, me).start()
     sibling_note(me).start()
+
+    fetch.wait()
+    for j in range(block_total):
+        b_ref[j] = raw[:, :, BLK * j:BLK * (j + 1)].reshape(b_ref.shape[1:])
 
     def window_of(which):
         return jnp.maximum(jnp.min(notes[pl.ds(2 * which, 2)]), 0)
@@ -166,22 +179,27 @@
     depth = occ_local * auxiliary
     block_total = orbitals // BLK
     slots = tile_pairs.shape[0]
-    blocks = b_factor.reshape(depth, block_total, BLK).transpose(1, 0, 2)
     phases = phase_lists(chips)
     return pl.pallas_call(
         functools.partial(kernel, chips, phases),
         out_shape=jax.ShapeDtypeStruct((slots, BLK, BLK), jnp.float32),
         in_specs=[
-            pl.BlockSpec(memory_space=pltpu.SMEM),
-            pl.BlockSpec(memory_space=pltpu.SMEM),
-            pl.BlockSpec(memory_space=pltpu.VMEM),
+            pl.BlockSpec(memory_space=pltpu.HBM),
+            pl.BlockSpec(memory_space=pltpu.HBM),
+            pl.BlockSpec(memory_space=pltpu.HBM),
         ],
         out_specs=pl.BlockSpec(memory_space=pltpu.VMEM),
         scratch_shapes=[
+            pltpu.SMEM((2, slots), jnp.int32),
+            pltpu.SMEM((1,), jnp.int32),
+            pltpu.VMEM(b_factor.shape, jnp.bfloat16),
+            pltpu.VMEM((block_total, depth, BLK), jnp.bfloat16),
             pltpu.VMEM((1, BLK), jnp.int32),
             pltpu.VMEM((devices, 1, BLK), jnp.int32),
             pltpu.VMEM((chips, 2, HALF, depth, BLK), jnp.bfloat16),
             *[pltpu.VMEM((len(group), 2, WINDOW, depth, BLK), jnp.bfloat16) for group in phases],
+            pltpu.SemaphoreType.DMA((2,)),
+            pltpu.SemaphoreType.DMA,
             pltpu.SemaphoreType.DMA((chips, 2)),
             pltpu.SemaphoreType.DMA((chips, 2)),
             pltpu.SemaphoreType.DMA((chips, 2)),
@@ -190,8 +208,8 @@
             pltpu.SemaphoreType.DMA((chips, 2)),
         ],
         compiler_params=pltpu.CompilerParams(
-            collective_id=0, has_side_effects=True, vmem_limit_bytes=32 * 1024 * 1024),
-    )(tile_pairs.T, tile_count, blocks)
+            collective_id=0, has_side_effects=True, vmem_limit_bytes=60 * 1024 * 1024),
+    )(tile_pairs.T, tile_count, b_factor)
 
 
 def solution(mesh):

time: 44.3 us -> 42.9 us (0.968)
  local copies, waits for them, and re-layouts: 4.18 us -> 2.3 us
    reshape x2 -> x0, local copies, waits for them, and re-layouts: 2.53 us -> none  [shards(): blocks = b_factor.reshape(depth, block_total, BLK).transpose(1, 0, 2)]
    unnamed x3 -> x1, local copies, waits for them, and re-layouts: 1.65 us -> 2.3 us
    pallas_call x1, Pallas kernels: 39.2 us -> 39.6 us  [shards(): pl.pallas_call(functools.partial(kernel, chips, phases), out_shape=jax.Sh...]
where the time goes in v3:
time: 42.9 us; the launch traced here: 42.6 us
  Pallas kernels  39.6 us (92%)
  local copies, waits for them, and re-layouts  2.3 us (5%)
  between operations  0.66 us (2%)
    pallas_call x1, Pallas kernels, shards(): pl.pallas_call(functools.partial(kernel, chips, phases), out_shape=jax.Sh...  39.6 us
    unnamed x1, local copies, waits for them, and re-layouts  2.3 us

profile of v3, /device:TPU:13, one launch (start us, length us, event | category | flops | bytes accessed | tf_op | source)
XLA Modules:
  0.0 42.6 jit_solution(11833374017784732121)
XLA Ops:
  0.7 39.6 %shard_map.37 = f32[16,128,128]{2,1,0:T(8,128)} custom-call(s32[2,16]{1,0:T(2,128)} %bitcast.1, s32[1]{0:T(128)S(6)} %copy.5.count_hbm, bf16[32,2,8192]{2,1,0:T(2,128)(2,1)} %b_hbm.1), custom_call_target="tpu_custom_call" | custom-call | tf_op jit(solution)/shard_map/pallas_call | solution.py:183
  40.3 2.3 %copy.6 = f32[16,128,128]{2,1,0:T(8,128)} copy(f32[16,128,128]{2,1,0:T(8,128)} %shard_map.37) | data formatting | bytes 2097152

commit v4 on v3

--- a/solution.py
+++ b/solution.py
@@ -28,7 +28,7 @@
     return [first, [d for d in range(half, chips) if d not in first]]
 
 
-def kernel(chips, phases, pairs_hbm, count_hbm, b_hbm, out_ref, pairs_ref, count_ref, raw, b_ref, note, notes, send, *rest):
+def kernel(chips, phases, pairs_hbm, count_ref, b_hbm, out_ref, pairs_ref, raw, b_ref, note, notes, send, *rest):
     recvs = rest[:len(phases)]
     small_sem, raw_sem, note_send, note_recv, data_send, data_recv, pass_send, pass_recv = rest[len(phases):]
     me = lax.axis_index("ao")
@@ -39,12 +39,8 @@
     block_total = b_ref.shape[0]
     where_of = {d: (p, i) for p, group in enumerate(phases) for i, d in enumerate(group)}
 
-    small = [
-        pltpu.make_async_copy(pairs_hbm, pairs_ref, small_sem.at[0]),
-        pltpu.make_async_copy(count_hbm, count_ref, small_sem.at[1]),
-    ]
-    for copy in small:
-        copy.start()
+    small = pltpu.make_async_copy(pairs_hbm, pairs_ref, small_sem)
+    small.start()
     barrier = pltpu.get_barrier_semaphore()
 
     def greet(step, carry):
@@ -56,8 +52,7 @@
     fetch = pltpu.make_async_copy(b_hbm, raw, raw_sem)
     fetch.start()
 
-    for copy in small:
-        copy.wait()
+    small.wait()
     count = count_ref[0]
     lowest = jnp.int32(block_total - WINDOW)
     for t in range(slots):
@@ -180,25 +175,25 @@
     block_total = orbitals // BLK
     slots = tile_pairs.shape[0]
     phases = phase_lists(chips)
+    in_hbm = functools.partial(pltpu.with_memory_space_constraint, memory_space=pltpu.HBM)
     return pl.pallas_call(
         functools.partial(kernel, chips, phases),
         out_shape=jax.ShapeDtypeStruct((slots, BLK, BLK), jnp.float32),
         in_specs=[
             pl.BlockSpec(memory_space=pltpu.HBM),
-            pl.BlockSpec(memory_space=pltpu.HBM),
+            pl.BlockSpec(memory_space=pltpu.SMEM),
             pl.BlockSpec(memory_space=pltpu.HBM),
         ],
         out_specs=pl.BlockSpec(memory_space=pltpu.VMEM),
         scratch_shapes=[
             pltpu.SMEM((2, slots), jnp.int32),
-            pltpu.SMEM((1,), jnp.int32),
             pltpu.VMEM(b_factor.shape, jnp.bfloat16),
             pltpu.VMEM((block_total, depth, BLK), jnp.bfloat16),
             pltpu.VMEM((1, BLK), jnp.int32),
             pltpu.VMEM((devices, 1, BLK), jnp.int32),
             pltpu.VMEM((chips, 2, HALF, depth, BLK), jnp.bfloat16),
             *[pltpu.VMEM((len(group), 2, WINDOW, depth, BLK), jnp.bfloat16) for group in phases],
-            pltpu.SemaphoreType.DMA((2,)),
+            pltpu.SemaphoreType.DMA,
             pltpu.SemaphoreType.DMA,
             pltpu.SemaphoreType.DMA((chips, 2)),
             pltpu.SemaphoreType.DMA((chips, 2)),
@@ -208,8 +203,8 @@
             pltpu.SemaphoreType.DMA((chips, 2)),
         ],
         compiler_params=pltpu.CompilerParams(
-            collective_id=0, has_side_effects=True, vmem_limit_bytes=60 * 1024 * 1024),
-    )(tile_pairs.T, tile_count, b_factor)
+            collective_id=0, has_side_effects=True, vmem_limit_bytes=32 * 1024 * 1024),
+    )(in_hbm(tile_pairs.T), tile_count, in_hbm(b_factor))
 
 
 def solution(mesh):

time: 42.9 us -> 40.5 us (0.944)
  local copies, waits for them, and re-layouts: 2.3 us -> 0.97 us
  Pallas kernels: 39.6 us -> 38.6 us
    unnamed x1, local copies, waits for them, and re-layouts: 2.3 us -> 0.97 us
    pallas_call x1, Pallas kernels: 39.6 us -> 38.6 us  [shards(): pl.pallas_call(functools.partial(kernel, chips, phases), out_shape=jax.Sh...]
where the time goes in v4:
time: 40.5 us; the launch traced here: 40.3 us
  Pallas kernels  38.6 us (95%)
  local copies, waits for them, and re-layouts  0.97 us (2%)
  between operations  0.66 us (2%)
    pallas_call x1, Pallas kernels, shards(): pl.pallas_call(functools.partial(kernel, chips, phases), out_shape=jax.Sh...  38.6 us
    unnamed x1, local copies, waits for them, and re-layouts  0.97 us

profile of v4, /device:TPU:13, one launch (start us, length us, event | category | flops | bytes accessed | tf_op | source)
XLA Modules:
  0.0 40.3 jit_solution(7258027837982607255)
XLA Ops:
  0.7 38.6 %shard_map.37 = f32[16,128,128]{2,1,0:T(8,128)S(1)} custom-call(s32[2,16]{1,0:T(2,128)} %bitcast.1, s32[1]{0:T(128)S(6)} %copy.5.count_ref, bf16[32,2,8192]{2,1,0:T(2,128)(2,1)} %b_hbm.1), custom_call_target="tpu_custom_call" | custom-call | tf_op jit(solution)/shard_map/pallas_call | solution.py:179
  39.3 1.0 %copy.6 = f32[16,128,128]{2,1,0:T(8,128)} copy(f32[16,128,128]{2,1,0:T(8,128)S(1)} %shard_map.37) | data formatting | bytes 2097152
